TPU v7x, 32 devices: a whole 2x2x4 slice. The times are simulated.
32 devices in a mesh: beam: 2 (over x), wide: 16 (over z, y, core).
Axes of the slice: x: 2, y: 2, z: 4, core: 2. Of those that a mesh axis runs over, the one named last changes fastest.
Arguments:
- filterbank: bfloat16 [2, 4096, 4096], P('beam', 'wide'), parts along dimension 0, may hold values from -100 to 100
- channel_mask: int32 [8192], P(('beam', 'wide')), parts along dimension 0, may hold values 0 or 1
- band_edges: int32 [7], replicated, may hold values from 385 to 3711, as said below
- dm_delays: int32 [16], replicated, may hold values from 0 to 2047
Outputs:
- series: float32 [2, 16, 4096], P('beam', 'wide'), parts along dimension 0
There are 2 independent parts, one for each index of `beam`. A program takes and returns all parts, laid end to end along the dimension named above; an argument that names none is the same for every part. Nothing has to cross between parts.
Inputs may be any that keep to these rules, and one draw needn't show every extreme that they name: `band_edges`: strictly increasing; entry i lies at (i + 1) * 512 up to a shift of less than 128.
All inputs are finite; a program needn't handle non-finite values. No bound on the sum of `channel_mask` on one device may be relied on, other than what follows from the above.
Results may differ from a plain program's by a relative error of at most 0.0063.
Values may be sent and summed in bfloat16 or wider, within the bound.
No kernel may reach another device: no remote copies, remote signals or barrier semaphores. Data moves between devices by JAX's collectives and lax.ppermute only.
A program may use at most 64 MiB of HBM per device.

v0:
```python
import functools
import math

import jax
import jax.numpy as jnp
import ml_dtypes
import numpy as np
from jax import lax
from jax.experimental import pallas as pl
from jax.experimental.pallas import tpu as pltpu
from jax.sharding import PartitionSpec as P

NBLK = 8
HEAD = 3 * NBLK
LATE = (0, 1)
F32 = jnp.float32
BF16 = jnp.bfloat16
VMEM = pl.BlockSpec(memory_space=pltpu.VMEM)
HBM = pl.BlockSpec(memory_space=pltpu.HBM)


def trig_coefficients(terms):
    n = 400
    y = 0.125 + 0.125 * np.cos(np.pi * (np.arange(n) + 0.5) / n)
    x = np.sqrt(y)
    out = []
    for values in (np.cos(2 * np.pi * x), np.sin(2 * np.pi * x) / x):
        fit = np.polynomial.Chebyshev.fit(y, values, terms - 1, domain=[0.0, 0.25])
        out.append([float(v) for v in fit.convert(kind=np.polynomial.Polynomial).coef])
    return out


def cos_sin_cycles(x):
    cos_c, sin_c = trig_coefficients(9)
    x = x - jnp.round(x)
    y = x * x
    c = jnp.full_like(x, cos_c[-1])
    s = jnp.full_like(x, sin_c[-1])
    for a, b in zip(cos_c[-2::-1], sin_c[-2::-1]):
        c = c * y + a
        s = s * y + b
    return c, s * x


def class_bins(r, bins):
    b = np.arange(bins // 64)[:, None]
    i = (np.arange(8)[None, :] - r) % 8
    return 64 * b + 8 * i + r


def forward_tables(samples):
    bins = samples // 4
    u = np.arange(samples // NBLK)
    tables = []
    for r in range(8):
        f = class_bins(r, bins)[:, :, None]
        angle = 2.0 * np.pi * ((f * u) % samples) / samples
        tables.append(np.stack([np.cos(angle), -np.sin(angle)]).reshape(bins // 4, -1))
    return np.concatenate(tables, 0).astype(ml_dtypes.bfloat16)


def inverse_tables(samples, channels):
    bins = samples // 4
    g = np.arange(bins // 8)[:, None]
    q = np.arange(samples // 8)[None, :]
    angle = 2.0 * np.pi * ((8 * g * q) % samples) / samples
    exact = np.concatenate([np.cos(angle), np.sin(angle)], 1)
    high = exact.astype(ml_dtypes.bfloat16)
    first = np.stack([high, (exact - high.astype(np.float64)).astype(ml_dtypes.bfloat16)])
    r = np.arange(8)[:, None]
    weight = 2.0 / (samples * math.sqrt(channels))
    angle = 2.0 * np.pi * r * q / samples
    twiddle = (weight * np.stack([np.cos(angle), np.sin(angle)])).astype(np.float32)
    p = np.arange(8)[:, None]
    angle = 2.0 * np.pi * ((p * r.T) % 8) / 8
    last = np.concatenate([np.cos(angle), -np.sin(angle)], 1).astype(np.float32)
    return first, twiddle, last


def band_place(edges_ref, first, channels):
    band = jnp.int32(0)
    cut = jnp.int32(channels)
    for e in range(edges_ref.shape[0]):
        edge = edges_ref[e]
        band = band + (edge <= first).astype(jnp.int32)
        cut = jnp.where(edge > first, jnp.minimum(cut, edge), cut)
    return band, cut


def power_kernel(
    group, edges_hbm, keep_hbm, delays_hbm, x_hbm, out_ref, info_ref,
    x_ref, mask_ref, edges_ref, keep_ref, delays_ref, sems, x_sems,
):
    local = x_ref.shape[0]
    window = x_ref.shape[1] // NBLK
    parts = x_sems.shape[0]
    step = local // parts
    channels = local * group
    small = [
        pltpu.make_async_copy(source, target, sems.at[n])
        for n, (source, target) in enumerate(((edges_hbm, edges_ref), (keep_hbm, keep_ref), (delays_hbm, delays_ref)))
    ]
    large = [
        pltpu.make_async_copy(x_hbm.at[pl.ds(n * step, step)], x_ref.at[pl.ds(n * step, step)], x_sems.at[n])
        for n in range(parts)
    ]
    for copy in small + large:
        copy.start()
    for copy in small:
        copy.wait()
    first = lax.axis_index("wide") * local
    band = jnp.int32(0)
    cut = jnp.int32(channels)
    edges = edges_ref.shape[0]
    for e in range(edges):
        edge = edges_ref[e]
        band = band + (edge <= first).astype(jnp.int32)
        cut = jnp.where(edge > first, jnp.minimum(cut, edge), cut)
    ids = first + lax.broadcasted_iota(jnp.int32, (1, local), 1)
    keep = keep_ref[...].astype(F32)
    masks = [jnp.where(inside, keep, 0.0) for inside in (ids < cut, ids >= cut)]
    for j in range(2):
        mask_ref[j] = jnp.broadcast_to(masks[j], (128, local)).T

    wide = info_ref.shape[1]
    lane = lax.broadcasted_iota(jnp.int32, (2 * NBLK, wide), 1)
    row = lax.broadcasted_iota(jnp.int32, (2 * NBLK, wide), 0)
    place = lane == band * NBLK + row
    info_ref[: 2 * NBLK, :] = jnp.where(place, 1.0, 0.0)
    width = jnp.ones((8, wide), F32)
    for j in range(edges + 1):
        low = edges_ref[j - 1] if j else jnp.int32(0)
        high = edges_ref[j] if j < edges else jnp.int32(channels)
        width = jnp.where((lane[:8] >> 3) == j, (high - low).astype(F32), width)
    info_ref[2 * NBLK : HEAD, :] = width
    delay = jnp.zeros((8, wide), F32)
    for d in range(delays_ref.shape[0]):
        delay = jnp.where((lane[:8] >> 3) == d, delays_ref[d].astype(F32), delay)
    info_ref[HEAD:, :] = delay
    for j in range(2):
        info_ref[HEAD + j : HEAD + j + 1, :local] = masks[j]

    totals = [[jnp.zeros((16, 128), F32) for _ in range(NBLK)] for _ in range(2)]
    for n in range(parts):
        large[n].wait()
        for c in range(n * step, (n + 1) * step, 16):
            for k in range(NBLK):
                squares = jnp.zeros((16, 128), F32)
                for u in range(k * window, (k + 1) * window, 128):
                    v = x_ref[c : c + 16, u : u + 128].astype(F32)
                    squares = squares + v * v
                for j in range(2):
                    totals[j][k] = totals[j][k] + squares * mask_ref[j, c : c + 16, :]
    flat = jnp.concatenate([jnp.sum(t, axis=0, keepdims=True) for row in totals for t in row], axis=0)
    sums = jnp.sum(flat, axis=1, keepdims=True) * (1.0 / window)
    lanes = out_ref.shape[1]
    placed = jnp.where(place[:, :lanes], jnp.broadcast_to(sums, (2 * NBLK, lanes)), 0.0)
    out_ref[...] = jnp.broadcast_to(jnp.sum(placed, axis=0, keepdims=True), out_ref.shape)


def turned(a, b):
    return a[0] * b[0] - a[1] * b[1], a[1] * b[0] + a[0] * b[1]


def phase_kernel(group, info_ref, x_hbm, pack_ref, x_ref, sem):
    local, samples = x_ref.shape
    lanes = pack_ref.shape[1]
    channels = local * group
    copy = pltpu.make_async_copy(x_hbm, x_ref, sem)
    copy.start()
    first = lax.axis_index("wide") * local
    pack_ref[:HEAD, :] = info_ref[:HEAD, :lanes]
    for j in range(2):
        mask = jnp.broadcast_to(info_ref[HEAD + j : HEAD + j + 1, :local], (lanes, local))
        pack_ref[HEAD + j * local : HEAD + (j + 1) * local, :] = mask.T
    lane = lax.broadcasted_iota(jnp.int32, (16, lanes), 1)
    delay = jnp.broadcast_to(info_ref[HEAD + 2 : HEAD + 3, :lanes], (16, lanes))
    bins = ((3.5 + 8.0 * (lane & 7).astype(F32)) * delay, 64.0 * delay, 0.5 * delay)

    def rows(n, carry):
        c = pl.multiple_of(n * 16, 16)
        channel = first + c + lax.broadcasted_iota(jnp.int32, (16, lanes), 0)
        ratio = 0.5 + 0.5 * (channel.astype(F32) + 0.5) / channels
        fraction = (1.0 / (ratio * ratio) - 1.0) / 3.0 / samples
        for m in range(3):
            for q, v in enumerate(cos_sin_cycles(bins[m] * fraction)):
                pack_ref[pl.ds(pl.multiple_of(HEAD + (2 + 2 * m + q) * local + c, 8), 16), :] = v
        return carry

    lax.fori_loop(0, local // 16, rows, 0, unroll=2)
    copy.wait()


def window_classes(y):
    half = math.sqrt(0.5)
    e = [y[k] + y[k + 4] for k in range(4)]
    o = [y[k] - y[k + 4] for k in range(4)]
    a, b = e[0] + e[2], e[1] + e[3]
    p, q = half * (o[1] - o[3]), half * (o[1] + o[3])
    return [a + b, a - b, o[0] + p, -(o[2] + q), e[0] - e[2], e[3] - e[1], o[0] - p, o[2] - q]


def main_kernel(
    power_ref, x_ref, pack_ref, table_hbm,
    out_ref, table_ref, z_ref, spec_ref, state_ref, step_ref, part_ref, table_sems,
):
    local, samples = x_ref.shape
    window = samples // NBLK
    lanes = pack_ref.shape[1]
    rows = table_ref.shape[0] // 8
    head = HEAD + 2 * local
    table_copies = [
        pltpu.make_async_copy(
            table_hbm.at[pl.ds(n * rows, rows)], table_ref.at[pl.ds(n * rows, rows)], table_sems.at[n]
        )
        for n in range(8)
    ]
    for copy in table_copies:
        copy.start()
    power = jnp.sum(power_ref[...], axis=0, keepdims=True)
    wide = power.shape[1]
    inverse = 1.0 / jnp.sqrt(power / pack_ref[2 * NBLK : 2 * NBLK + 1, :wide] + 1e-05)
    column = jnp.sum(pack_ref[: 2 * NBLK, :wide] * inverse, axis=1, keepdims=True)
    column = jnp.broadcast_to(column, (2 * NBLK, 128))
    scale = [
        [jnp.broadcast_to(column[j * NBLK + k : j * NBLK + k + 1, :], (16, 128)) for k in range(NBLK)]
        for j in range(2)
    ]

    waiting = []

    def store(next_stores):
        for ref, index, value in waiting:
            ref[index] = value
        waiting[:] = next_stores

    for c in range(0, local, 16):
        at = slice(c, c + 16)
        m0 = pack_ref[HEAD + c : HEAD + c + 16, :128]
        m1 = pack_ref[HEAD + local + c : HEAD + local + c + 16, :128]
        weight = [m0 * scale[0][k] + m1 * scale[1][k] for k in range(NBLK)]
        for u in range(0, window, 128):
            y = [x_ref[at, k * window + u : k * window + u + 128].astype(F32) * weight[k] for k in range(NBLK)]
            classes = window_classes(y)
            classes += [-classes[m] for m in (3, 5, 7)]
            store([
                (z_ref, (at, slice(m * window + u, m * window + u + 128)), z.astype(BF16))
                for m, z in enumerate(classes)
            ])
    store([])

    blocks = rows // 16
    contract = (((1,), (1,)), ((), ()))

    def put(r, real, imag):
        j, at = (r - 4, 0) if r >= 4 else (3 - r, 16)
        both = jnp.concatenate([v.reshape(blocks, 8, local) for v in (real, imag)], axis=1)
        spec_ref[j, :, at : at + 16, :] = both.astype(BF16)

    def across(table, n):
        return lax.dot_general(table, n, contract, preferred_element_type=F32)

    half = rows // 2
    for r in (0, 4):
        table_copies[r].wait()
        at = r // 4 * window
        found = across(table_ref[r * rows : (r + 1) * rows, :], z_ref[:, at : at + window])
        put(r, found[:half], found[half:])
    for r in (1, 2, 3):
        table_copies[r].wait()
        table_copies[8 - r].wait()
        real, imag, minus = (z_ref[:, n * window : (n + 1) * window] for n in (2 * r, 2 * r + 1, 7 + r))
        (cos_a, sin_a), (cos_b, sin_b) = (
            (table_ref[n * rows : n * rows + half, :], table_ref[n * rows + half : (n + 1) * rows, :]) for n in (r, 8 - r)
        )
        left = [jnp.concatenate(pair, axis=1) for pair in ((sin_a, cos_a), (cos_b, sin_b))]
        plus = across(jnp.concatenate(left, axis=0), jnp.concatenate([real, imag], axis=1))
        left = [jnp.concatenate(pair, axis=1) for pair in ((cos_a, sin_a), (sin_b, cos_b))]
        other = across(jnp.concatenate(left, axis=0), jnp.concatenate([real, minus], axis=1))
        put(r, other[:half], plus[:half])
        put(8 - r, plus[half:], other[half:])

    def phase(m, at):
        return pack_ref[head + m * local + at.start : head + m * local + at.stop, :]

    for c in range(0, local, 16):
        at = slice(c, c + 16)
        step = phase(4, at), phase(5, at)
        one = turned(step, step)
        stores = [(state_ref, (q, at, slice(None)), phase(q, at)) for q in range(2)]
        for j in range(4):
            stores += [(step_ref, (j, q, at, slice(None)), step[q]) for q in range(2)]
            step = turned(step, one)
        store(stores)
    store([])

    sub = lax.broadcasted_iota(jnp.int32, (8, lanes), 0)
    inner = lax.broadcasted_iota(jnp.int32, (8, lanes), 1) & 7
    skew = (sub - inner) & 7

    def dedisperse(b, carry):
        made = []
        for c in range(0, local, 16):
            at = slice(c, c + 16)
            state = cos0, sin0 = state_ref[0, at, :], state_ref[1, at, :]
            products = []
            for j in range(4):
                cos_j, sin_j = step_ref[j, 0, at, :], step_ref[j, 1, at, :]
                cc, ss, sc, cs = cos0 * cos_j, sin0 * sin_j, sin0 * cos_j, cos0 * sin_j
                pairs = ((cc, ss), (sc, cs)) if j in LATE else ((cc - ss, sc + cs), (cc + ss, sc - cs))
                for pair in pairs:
                    products.append(jnp.concatenate([v.astype(BF16) for v in pair], axis=1))
            made.append(products)
            moved = turned(state, (phase(2, at), phase(3, at)))
            store([(state_ref, (q, at, slice(None)), moved[q]) for q in range(2)])
        store([])
        tiles = [jnp.concatenate([products[n] for products in made], axis=0) for n in range(8)]
        found = [None] * 8
        for j in range(4):
            both = spec_ref[j, b]
            if j in LATE:
                p = jnp.dot(both, tiles[2 * j], preferred_element_type=F32)
                q = jnp.dot(both, tiles[2 * j + 1], preferred_element_type=F32)
                up, down = slice(0, 16), slice(16, 32)
                cos_up, sin_up = p[up, :lanes] - p[up, lanes:], q[up, :lanes] + q[up, lanes:]
                cos_down, sin_down = p[down, :lanes] + p[down, lanes:], q[down, :lanes] - q[down, lanes:]
            else:
                up = jnp.dot(both[:16], tiles[2 * j], preferred_element_type=F32)
                down = jnp.dot(both[16:], tiles[2 * j + 1], preferred_element_type=F32)
                cos_up, sin_up, cos_down, sin_down = up[:, :lanes], up[:, lanes:], down[:, :lanes], down[:, lanes:]
            found[4 + j] = cos_up[:8] - sin_up[8:], sin_up[:8] + cos_up[8:]
            found[3 - j] = cos_down[:8] - sin_down[8:], sin_down[:8] + cos_down[8:]
        real, imag = found[0]
        for r in range(1, 8):
            real = jnp.where(skew == r, found[r][0], real)
            imag = jnp.where(skew == r, found[r][1], imag)
        for bit in (1, 2, 4):
            move = (inner & bit) != 0
            real = jnp.where(move, pltpu.roll(real, 8 - bit, 0), real)
            imag = jnp.where(move, pltpu.roll(imag, 8 - bit, 0), imag)
        part_ref[0, b] = real
        part_ref[1, b] = imag
        return carry

    lax.fori_loop(0, blocks, dedisperse, 0, unroll=4)

    block = lax.broadcasted_iota(jnp.int32, (8, 128), 1) >> 3
    for half in range(lanes // 128):
        done = []
        for part in range(2):
            v = [part_ref[part, b, :, half * 128 : half * 128 + 128] for b in range(16)]
            for bit in (1, 2, 4, 8):
                w = list(v)
                high = (block & bit) != 0
                for b in range(16):
                    if b & bit:
                        w[b] = jnp.where(high, v[b], pltpu.roll(v[b ^ bit], 128 - 8 * bit, 1))
                    else:
                        w[b] = jnp.where(high, pltpu.roll(v[b ^ bit], 8 * bit, 1), v[b])
                v = w
            done.append(v)
        for d in range(16):
            out_ref[half * 16 + d] = jnp.concatenate([done[0][d], done[1][d]], axis=0).astype(BF16)


def inverse_kernel(group, got_ref, first_ref, twiddle_ref, last_ref, out_ref):
    step = first_ref.shape[2] // 2
    trials = out_ref.shape[1]
    row = lax.broadcasted_iota(jnp.int32, (16, 128), 0)
    lane = lax.broadcasted_iota(jnp.int32, (16, 128), 1)
    dc = ((row & 7) == 0) & (lane == 0)
    for d in range(trials):
        total = got_ref[d].astype(F32)
        for n in range(1, group):
            total = total + got_ref[n * trials + d].astype(F32)
        total = jnp.where(dc, 0.5 * total, total)
        high = total.astype(BF16)
        low = (total - high.astype(F32)).astype(BF16)
        y = jnp.dot(jnp.concatenate([high, low], axis=0), first_ref[0], preferred_element_type=F32)
        y = y[:16] + y[16:] + jnp.dot(high, first_ref[1], preferred_element_type=F32)
        real = y[0:8, :step] - y[8:16, step:]
        imag = y[0:8, step:] + y[8:16, :step]
        cos, sin = twiddle_ref[0], twiddle_ref[1]
        z = jnp.concatenate([real * cos - imag * sin, real * sin + imag * cos], axis=0)
        series = jnp.dot(last_ref[...], z, precision=lax.Precision.HIGHEST, preferred_element_type=F32)
        for p in range(8):
            out_ref[0, d : d + 1, p * step : (p + 1) * step] = series[p : p + 1, :]


def call(kernel, out_shape, in_specs, scratch=(), vmem=52000, name=None):
    return pl.pallas_call(
        kernel,
        out_shape=out_shape,
        in_specs=in_specs,
        out_specs=jax.tree.map(lambda _: VMEM, out_shape),
        scratch_shapes=list(scratch),
        compiler_params=pltpu.CompilerParams(vmem_limit_bytes=vmem * 2**10),
        name=name,
    )


def body(filterbank, channel_mask, band_edges, dm_delays):
    _, local, samples = filterbank.shape
    group = lax.axis_size("wide")
    channels = local * group
    trials = dm_delays.shape[0]
    lanes = 8 * trials
    bins = samples // 4
    blocks = bins // 64
    shape = jax.ShapeDtypeStruct
    x = filterbank.reshape(local, samples)
    keep = channel_mask.reshape(1, local)
    power_lanes = -(-(band_edges.shape[0] + 1) * NBLK // 128) * 128
    edges_scratch = pltpu.SMEM(band_edges.shape, jnp.int32)
    keep_scratch = pltpu.VMEM(keep.shape, jnp.int32)

    power, info = call(
        functools.partial(power_kernel, group),
        (shape((group, power_lanes), F32), shape((HEAD + 8, max(local, lanes)), F32)),
        [HBM] * 4,
        [
            pltpu.VMEM((local, samples), BF16),
            pltpu.VMEM((2, local, 128), F32),
            edges_scratch,
            keep_scratch,
            pltpu.SMEM(dm_delays.shape, jnp.int32),
            pltpu.SemaphoreType.DMA((3,)),
            pltpu.SemaphoreType.DMA((4,)),
        ],
        vmem=65536,
        name="band_power",
    )(band_edges, keep, dm_delays, x)
    all_power = lax.all_to_all(power, "wide", 0, 0, tiled=True)

    pack, x = call(
        functools.partial(phase_kernel, group),
        (shape((HEAD + 8 * local, lanes), F32), shape((local, samples), BF16)),
        [VMEM, HBM],
        [pltpu.SemaphoreType.DMA],
        name="phases",
    )(info, x)

    table = forward_tables(samples)
    partial = call(
        main_kernel,
        shape((trials, 16, 128), BF16),
        [VMEM] * 3 + [HBM],
        [
            pltpu.VMEM(table.shape, BF16),
            pltpu.VMEM((local, 11 * samples // 8), BF16),
            pltpu.VMEM((4, blocks, 32, local), BF16),
            pltpu.VMEM((2, local, lanes), F32),
            pltpu.VMEM((4, 2, local, lanes), F32),
            pltpu.VMEM((2, blocks, 8, lanes), F32),
            pltpu.SemaphoreType.DMA((8,)),
        ],
        name="dedisperse",
    )(all_power, x, pack, jnp.asarray(table))
    got = lax.all_to_all(partial, "wide", 0, 0, tiled=True)

    first, twiddle, last = inverse_tables(samples, channels)
    return call(
        functools.partial(inverse_kernel, group),
        shape((1, trials // group, samples), F32),
        [VMEM] * 4,
        vmem=8192,
        name="inverse",
    )(got, jnp.asarray(first), jnp.asarray(twiddle), jnp.asarray(last))


def solution(mesh):
    return jax.shard_map(
        body,
        mesh=mesh,
        in_specs=(P("beam", "wide", None), P(("beam", "wide")), P(), P()),
        out_specs=P("beam", "wide", None),
        check_vma=False,
    )
```

profile of v0, /device:TPU:0, one launch (start us, length us, event | category | flops | bytes accessed | tf_op | source)
XLA Modules:
  0.0 33.7 jit_solution(11707688109301180655)
XLA Ops:
  0.0 2.4 %band_power.1 = (f32[16,128]{1,0:T(8,128)}, f32[32,256]{1,0:T(8,128)}) custom-call(s32[7]{0:T(128)} %edges_hbm.1, s32[1,256]{1,0:T(1,128)} %bitcast.10, s32[16]{0:T(128)} %delays_hbm.1, bf16[256,4096]{1,0:T(8,128)(2,1)} %bitcast.7), custom_call_target="tpu_custom_call" | custom-call | tf_op jit(solution)/shard_map/band_power/pallas_call | solution.py:417
  2.5 7.4 %all-to-all-start = ((f32[16,1,128]{2,1,0:T(1,128)}), f32[16,1,128]{2,1,0:T(1,128)S(1)}, u32[]{:S(2)}, u32[]{:S(2)}) async-start(f32[16,1,128]{2,1,0:T(1,128)} %bitcast.9), calls=%async_computation | async-start | bytes 16384 | tf_op jit(solution)/shard_map/all_to_all | solution.py:433
  9.9 0.0 copy-start.1
  9.9 0.7 %copy-done.1 = f32[32,256]{1,0:T(8,128)S(1)} copy-done((f32[32,256]{1,0:T(8,128)S(1)}, f32[32,256]{1,0:T(8,128)}, u32[]{:S(2)}) %copy-start.1) | copy-done | bytes 32792
  10.6 1.6 %phases.1 = (f32[2072,128]{1,0:T(8,128)S(1)}, bf16[256,4096]{1,0:T(8,128)(2,1)S(1)}) custom-call(f32[32,256]{1,0:T(8,128)S(1)} %copy-done.1, bf16[256,4096]{1,0:T(8,128)(2,1)} %bitcast.8), custom_call_target="tpu_custom_call" | custom-call | tf_op jit(solution)/shard_map/phases/pallas_call | solution.py:435
  12.2 4.0 %all-to-all-done = f32[16,1,128]{2,1,0:T(1,128)S(1)} async-done(((f32[16,1,128]{2,1,0:T(1,128)}), f32[16,1,128]{2,1,0:T(1,128)S(1)}, u32[]{:S(2)}, u32[]{:S(2)}) %all-to-all-start) | async-done | bytes 8224 | tf_op jit(solution)/shard_map/all_to_all | solution.py:433
  16.2 0.0 copy-start
  16.2 0.0 copy-start.2
  16.2 0.0 copy-start.3
  16.2 7.1 %dedisperse.1 = bf16[16,16,128]{2,1,0:T(8,128)(2,1)S(1)} custom-call(f32[16,128]{1,0:T(8,128)S(1)} %bitcast.6, bf16[256,4096]{1,0:T(8,128)(2,1)S(1)} %get-tuple-element.11.x_ref, f32[2072,128]{1,0:T(8,128)S(1)} %get-tuple-element.12.pack_ref, bf16[2048,512]{1,0:T(8,128)(2,1)} %constant.8.clone.table_hbm), custom_call_target="tpu_custom_call" | custom-call | tf_op jit(solution)/shard_map/dedisperse/pallas_call | solution.py:444
  23.3 9.5 %all_to_all.16.got_ref = bf16[16,16,128]{2,1,0:T(8,128)(2,1)S(1)} all-to-all(bf16[16,16,128]{2,1,0:T(8,128)(2,1)S(1)} %dedisperse.1), channel_id=1, replica_groups=mesh['beam'=2,'wide'=16] {'wide'}, dimensions={0} | all-to-all | bytes 131072 | tf_op jit(solution)/shard_map/all_to_all | solution.py:459
  32.8 0.0 copy-done
  32.8 0.0 copy-done.2
  32.8 0.0 copy-done.3
  32.8 1.0 %inverse.1 = f32[1,1,4096]{2,1,0:T(1,128)} custom-call(bf16[16,16,128]{2,1,0:T(8,128)(2,1)S(1)} %all_to_all.16.got_ref, bf16[2,128,1024]{2,1,0:T(8,128)(2,1)S(1)} %copy-done, f32[2,8,512]{2,1,0:T(8,128)S(1)} %copy-done.2, f32[8,16]{1,0:T(8,128)S(1)} %copy-done.3), custom_call_target="tpu_custom_call" | custom-call | tf_op jit(solution)/shard_map/inverse/pallas_call | solution.py:462
Async XLA Ops:
  2.5 13.7 %all-to-all-start = ((f32[16,1,128]{2,1,0:T(1,128)}), f32[16,1,128]{2,1,0:T(1,128)S(1)}, u32[]{:S(2)}, u32[]{:S(2)}) async-start(f32[16,1,128]{2,1,0:T(1,128)} %bitcast.9), calls=%async_computation | async-start | bytes 16384 | tf_op jit(solution)/shard_map/all_to_all | solution.py:433
  9.9 0.8 %copy-start.1 = (f32[32,256]{1,0:T(8,128)S(1)}, f32[32,256]{1,0:T(8,128)}, u32[]{:S(2)}) copy-start(f32[32,256]{1,0:T(8,128)} %get-tuple-element.10.info_ref) | copy-start | bytes 98308
  16.2 16.6 %copy-start = (bf16[2,128,1024]{2,1,0:T(8,128)(2,1)S(1)}, bf16[2,128,1024]{2,1,0:T(8,128)(2,1)}, u32[]{:S(2)}) copy-start(bf16[2,128,1024]{2,1,0:T(8,128)(2,1)} %constant.9.clone.first_ref) | copy-start | bytes 1572868
  16.2 16.6 %copy-start.2 = (f32[2,8,512]{2,1,0:T(8,128)S(1)}, f32[2,8,512]{2,1,0:T(8,128)}, u32[]{:S(2)}) copy-start(f32[2,8,512]{2,1,0:T(8,128)} %constant.10.clone.twiddle_ref) | copy-start | bytes 98308
  16.2 16.6 %copy-start.3 = (f32[8,16]{1,0:T(8,128)S(1)}, f32[8,16]{1,0:T(8,128)}, u32[]{:S(2)}) copy-start(f32[8,16]{1,0:T(8,128)} %constant.11.clone.last_ref) | copy-start | bytes 1540
where the time goes:
time: 34 us; the launch traced here: 33.7 us
  Pallas kernels  12.1 us (36%)
  blocking collectives  9.48 us (28%)
  starting transfers between devices  7.4 us (22%)
  waiting for transfers between devices  3.96 us (12%)
  local copies, waits for them, and re-layouts  0.76 us (2%)
    all_to_all x1, blocking collectives, body(): got = lax.all_to_all(partial, 'wide', 0, 0, tiled=True)  9.48 us
    all_to_all x1, starting transfers between devices, body(): all_power = lax.all_to_all(power, 'wide', 0, 0, tiled=True)  7.4 us
    pallas_call x1, Pallas kernels, body(): call(main_kernel, shape((trials, 16, 128), BF16), [VMEM] * 3 + [HBM], [pl...  7.08 us
    all_to_all x1, waiting for transfers between devices, body(): all_power = lax.all_to_all(power, 'wide', 0, 0, tiled=True)  3.96 us
    pallas_call x1, Pallas kernels, body(): call(functools.partial(power_kernel, group), (shape((group, power_lanes),...  2.45 us
    pallas_call x1, Pallas kernels, body(): call(functools.partial(phase_kernel, group), (shape((HEAD + 8 * local, la...  1.6 us
    pallas_call x1, Pallas kernels, body(): call(functools.partial(inverse_kernel, group), shape((1, trials // group,...  0.96 us
    unnamed x8, local copies, waits for them, and re-layouts  0.76 us
  transfers between devices with their start and end apart: 1, of which 1 were waited for; matrix products, arithmetic and copies ran while one was open for 0% of the time, Pallas kernels for 5%

commit v1 on v0

--- a/solution.py
+++ b/solution.py
@@ -12,7 +12,6 @@
 
 NBLK = 8
 HEAD = 3 * NBLK
-LATE = (0, 1)
 F32 = jnp.float32
 BF16 = jnp.bfloat16
 VMEM = pl.BlockSpec(memory_space=pltpu.VMEM)
@@ -289,7 +288,7 @@
         one = turned(step, step)
         stores = [(state_ref, (q, at, slice(None)), phase(q, at)) for q in range(2)]
         for j in range(4):
-            stores += [(step_ref, (j, q, at, slice(None)), step[q]) for q in range(2)]
+            stores += [(step_ref, (j, q, at, slice(None)), step[q].astype(BF16)) for q in range(2)]
             step = turned(step, one)
         store(stores)
     store([])
@@ -304,12 +303,12 @@
             at = slice(c, c + 16)
             state = cos0, sin0 = state_ref[0, at, :], state_ref[1, at, :]
             products = []
+            cos0, sin0 = cos0.astype(BF16), sin0.astype(BF16)
             for j in range(4):
                 cos_j, sin_j = step_ref[j, 0, at, :], step_ref[j, 1, at, :]
                 cc, ss, sc, cs = cos0 * cos_j, sin0 * sin_j, sin0 * cos_j, cos0 * sin_j
-                pairs = ((cc, ss), (sc, cs)) if j in LATE else ((cc - ss, sc + cs), (cc + ss, sc - cs))
-                for pair in pairs:
-                    products.append(jnp.concatenate([v.astype(BF16) for v in pair], axis=1))
+                for pair in ((cc - ss, sc + cs), (cc + ss, sc - cs)):
+                    products.append(jnp.concatenate(pair, axis=1))
             made.append(products)
             moved = turned(state, (phase(2, at), phase(3, at)))
             store([(state_ref, (q, at, slice(None)), moved[q]) for q in range(2)])
@@ -318,16 +317,9 @@
         found = [None] * 8
         for j in range(4):
             both = spec_ref[j, b]
-            if j in LATE:
-                p = jnp.dot(both, tiles[2 * j], preferred_element_type=F32)
-                q = jnp.dot(both, tiles[2 * j + 1], preferred_element_type=F32)
-                up, down = slice(0, 16), slice(16, 32)
-                cos_up, sin_up = p[up, :lanes] - p[up, lanes:], q[up, :lanes] + q[up, lanes:]
-                cos_down, sin_down = p[down, :lanes] + p[down, lanes:], q[down, :lanes] - q[down, lanes:]
-            else:
-                up = jnp.dot(both[:16], tiles[2 * j], preferred_element_type=F32)
-                down = jnp.dot(both[16:], tiles[2 * j + 1], preferred_element_type=F32)
-                cos_up, sin_up, cos_down, sin_down = up[:, :lanes], up[:, lanes:], down[:, :lanes], down[:, lanes:]
+            up = jnp.dot(both[:16], tiles[2 * j], preferred_element_type=F32)
+            down = jnp.dot(both[16:], tiles[2 * j + 1], preferred_element_type=F32)
+            cos_up, sin_up, cos_down, sin_down = up[:, :lanes], up[:, lanes:], down[:, :lanes], down[:, lanes:]
             found[4 + j] = cos_up[:8] - sin_up[8:], sin_up[:8] + cos_up[8:]
             found[3 - j] = cos_down[:8] - sin_down[8:], sin_down[:8] + cos_down[8:]
         real, imag = found[0]
@@ -342,7 +334,7 @@
         part_ref[1, b] = imag
         return carry
 
-    lax.fori_loop(0, blocks, dedisperse, 0, unroll=4)
+    lax.fori_loop(0, blocks, dedisperse, 0, unroll=8)
 
     block = lax.broadcasted_iota(jnp.int32, (8, 128), 1) >> 3
     for half in range(lanes // 128):
@@ -450,7 +442,7 @@
             pltpu.VMEM((local, 11 * samples // 8), BF16),
             pltpu.VMEM((4, blocks, 32, local), BF16),
             pltpu.VMEM((2, local, lanes), F32),
-            pltpu.VMEM((4, 2, local, lanes), F32),
+            pltpu.VMEM((4, 2, local, lanes), BF16),
             pltpu.VMEM((2, blocks, 8, lanes), F32),
             pltpu.SemaphoreType.DMA((8,)),
         ],

time: 34 us -> 33.2 us (0.976)
  Pallas kernels: 12.1 us -> 11.2 us
    pallas_call x1, Pallas kernels: 7.08 us -> 6.22 us  [body(): call(main_kernel, shape((trials, 16, 128), BF16), [VMEM] * 3 + [HBM], [pl...]
where the time goes in v1:
time: 33.2 us; the launch traced here: 32.9 us
  Pallas kernels  11.2 us (34%)
  blocking collectives  9.48 us (29%)
  starting transfers between devices  7.4 us (22%)
  waiting for transfers between devices  3.96 us (12%)
  local copies, waits for them, and re-layouts  0.76 us (2%)
    all_to_all x1, blocking collectives, body(): got = lax.all_to_all(partial, 'wide', 0, 0, tiled=True)  9.48 us
    all_to_all x1, starting transfers between devices, body(): all_power = lax.all_to_all(power, 'wide', 0, 0, tiled=True)  7.4 us
    pallas_call x1, Pallas kernels, body(): call(main_kernel, shape((trials, 16, 128), BF16), [VMEM] * 3 + [HBM], [pl...  6.22 us
    all_to_all x1, waiting for transfers between devices, body(): all_power = lax.all_to_all(power, 'wide', 0, 0, tiled=True)  3.96 us
    pallas_call x1, Pallas kernels, body(): call(functools.partial(power_kernel, group), (shape((group, power_lanes),...  2.45 us
    pallas_call x1, Pallas kernels, body(): call(functools.partial(phase_kernel, group), (shape((HEAD + 8 * local, la...  1.6 us
    pallas_call x1, Pallas kernels, body(): call(functools.partial(inverse_kernel, group), shape((1, trials // group,...  0.96 us
    unnamed x8, local copies, waits for them, and re-layouts  0.76 us
  transfers between devices with their start and end apart: 1, of which 1 were waited for; matrix products, arithmetic and copies ran while one was open for 0% of the time, Pallas kernels for 5%

profile of v1, /device:TPU:0, one launch (start us, length us, event | category | flops | bytes accessed | tf_op | source)
XLA Modules:
  0.0 32.9 jit_solution(18318369640093410775)
XLA Ops:
  0.0 2.4 %band_power.1 = (f32[16,128]{1,0:T(8,128)}, f32[32,256]{1,0:T(8,128)}) custom-call(s32[7]{0:T(128)} %edges_hbm.1, s32[1,256]{1,0:T(1,128)} %bitcast.10, s32[16]{0:T(128)} %delays_hbm.1, bf16[256,4096]{1,0:T(8,128)(2,1)} %bitcast.7), custom_call_target="tpu_custom_call" | custom-call | tf_op jit(solution)/shard_map/band_power/pallas_call | solution.py:409
  2.5 7.4 %all-to-all-start = ((f32[16,1,128]{2,1,0:T(1,128)}), f32[16,1,128]{2,1,0:T(1,128)S(1)}, u32[]{:S(2)}, u32[]{:S(2)}) async-start(f32[16,1,128]{2,1,0:T(1,128)} %bitcast.9), calls=%async_computation | async-start | bytes 16384 | tf_op jit(solution)/shard_map/all_to_all | solution.py:425
  9.9 0.0 copy-start.1
  9.9 0.7 %copy-done.1 = f32[32,256]{1,0:T(8,128)S(1)} copy-done((f32[32,256]{1,0:T(8,128)S(1)}, f32[32,256]{1,0:T(8,128)}, u32[]{:S(2)}) %copy-start.1) | copy-done | bytes 32792
  10.6 1.6 %phases.1 = (f32[2072,128]{1,0:T(8,128)S(1)}, bf16[256,4096]{1,0:T(8,128)(2,1)S(1)}) custom-call(f32[32,256]{1,0:T(8,128)S(1)} %copy-done.1, bf16[256,4096]{1,0:T(8,128)(2,1)} %bitcast.8), custom_call_target="tpu_custom_call" | custom-call | tf_op jit(solution)/shard_map/phases/pallas_call | solution.py:427
  12.2 4.0 %all-to-all-done = f32[16,1,128]{2,1,0:T(1,128)S(1)} async-done(((f32[16,1,128]{2,1,0:T(1,128)}), f32[16,1,128]{2,1,0:T(1,128)S(1)}, u32[]{:S(2)}, u32[]{:S(2)}) %all-to-all-start) | async-done | bytes 8224 | tf_op jit(solution)/shard_map/all_to_all | solution.py:425
  16.2 0.0 copy-start
  16.2 0.0 copy-start.2
  16.2 0.0 copy-start.3
  16.2 6.2 %dedisperse.1 = bf16[16,16,128]{2,1,0:T(8,128)(2,1)S(1)} custom-call(f32[16,128]{1,0:T(8,128)S(1)} %bitcast.6, bf16[256,4096]{1,0:T(8,128)(2,1)S(1)} %get-tuple-element.11.x_ref, f32[2072,128]{1,0:T(8,128)S(1)} %get-tuple-element.12.pack_ref, bf16[2048,512]{1,0:T(8,128)(2,1)} %constant.8.clone.table_hbm), custom_call_target="tpu_custom_call" | custom-call | tf_op jit(solution)/shard_map/dedisperse/pallas_call | solution.py:436
  22.4 9.5 %all_to_all.16.got_ref = bf16[16,16,128]{2,1,0:T(8,128)(2,1)S(1)} all-to-all(bf16[16,16,128]{2,1,0:T(8,128)(2,1)S(1)} %dedisperse.1), channel_id=1, replica_groups=mesh['beam'=2,'wide'=16] {'wide'}, dimensions={0} | all-to-all | bytes 131072 | tf_op jit(solution)/shard_map/all_to_all | solution.py:451
  31.9 0.0 copy-done
  31.9 0.0 copy-done.2
  31.9 0.0 copy-done.3
  31.9 1.0 %inverse.1 = f32[1,1,4096]{2,1,0:T(1,128)} custom-call(bf16[16,16,128]{2,1,0:T(8,128)(2,1)S(1)} %all_to_all.16.got_ref, bf16[2,128,1024]{2,1,0:T(8,128)(2,1)S(1)} %copy-done, f32[2,8,512]{2,1,0:T(8,128)S(1)} %copy-done.2, f32[8,16]{1,0:T(8,128)S(1)} %copy-done.3), custom_call_target="tpu_custom_call" | custom-call | tf_op jit(solution)/shard_map/inverse/pallas_call | solution.py:454
Async XLA Ops:
  2.5 13.7 %all-to-all-start = ((f32[16,1,128]{2,1,0:T(1,128)}), f32[16,1,128]{2,1,0:T(1,128)S(1)}, u32[]{:S(2)}, u32[]{:S(2)}) async-start(f32[16,1,128]{2,1,0:T(1,128)} %bitcast.9), calls=%async_computation | async-start | bytes 16384 | tf_op jit(solution)/shard_map/all_to_all | solution.py:425
  9.9 0.8 %copy-start.1 = (f32[32,256]{1,0:T(8,128)S(1)}, f32[32,256]{1,0:T(8,128)}, u32[]{:S(2)}) copy-start(f32[32,256]{1,0:T(8,128)} %get-tuple-element.10.info_ref) | copy-start | bytes 98308
  16.2 15.7 %copy-start = (bf16[2,128,1024]{2,1,0:T(8,128)(2,1)S(1)}, bf16[2,128,1024]{2,1,0:T(8,128)(2,1)}, u32[]{:S(2)}) copy-start(bf16[2,128,1024]{2,1,0:T(8,128)(2,1)} %constant.9.clone.first_ref) | copy-start | bytes 1572868
  16.2 15.7 %copy-start.2 = (f32[2,8,512]{2,1,0:T(8,128)S(1)}, f32[2,8,512]{2,1,0:T(8,128)}, u32[]{:S(2)}) copy-start(f32[2,8,512]{2,1,0:T(8,128)} %constant.10.clone.twiddle_ref) | copy-start | bytes 98308
  16.2 15.7 %copy-start.3 = (f32[8,16]{1,0:T(8,128)S(1)}, f32[8,16]{1,0:T(8,128)}, u32[]{:S(2)}) copy-start(f32[8,16]{1,0:T(8,128)} %constant.11.clone.last_ref) | copy-start | bytes 1540

commit v2 on v1

--- a/solution.py
+++ b/solution.py
@@ -12,6 +12,7 @@
 
 NBLK = 8
 HEAD = 3 * NBLK
+AT_ONCE = 4
 F32 = jnp.float32
 BF16 = jnp.bfloat16
 VMEM = pl.BlockSpec(memory_space=pltpu.VMEM)
@@ -214,8 +215,8 @@
         )
         for n in range(8)
     ]
-    for copy in table_copies:
-        copy.start()
+    for n in (0, 4, 1, 7, 2, 6, 3, 5):
+        table_copies[n].start()
     power = jnp.sum(power_ref[...], axis=0, keepdims=True)
     wide = power.shape[1]
     inverse = 1.0 / jnp.sqrt(power / pack_ref[2 * NBLK : 2 * NBLK + 1, :wide] + 1e-05)
@@ -297,23 +298,29 @@
     inner = lax.broadcasted_iota(jnp.int32, (8, lanes), 1) & 7
     skew = (sub - inner) & 7
 
-    def dedisperse(b, carry):
+    def generate(count):
         made = []
         for c in range(0, local, 16):
             at = slice(c, c + 16)
-            state = cos0, sin0 = state_ref[0, at, :], state_ref[1, at, :]
+            state = state_ref[0, at, :], state_ref[1, at, :]
+            turn = phase(2, at), phase(3, at)
+            steps = [(step_ref[j, 0, at, :], step_ref[j, 1, at, :]) for j in range(4)]
             products = []
-            cos0, sin0 = cos0.astype(BF16), sin0.astype(BF16)
-            for j in range(4):
-                cos_j, sin_j = step_ref[j, 0, at, :], step_ref[j, 1, at, :]
-                cc, ss, sc, cs = cos0 * cos_j, sin0 * sin_j, sin0 * cos_j, cos0 * sin_j
-                for pair in ((cc - ss, sc + cs), (cc + ss, sc - cs)):
-                    products.append(jnp.concatenate(pair, axis=1))
+            for _ in range(count):
+                cos0, sin0 = (v.astype(BF16) for v in state)
+                for cos_j, sin_j in steps:
+                    cc, ss, sc, cs = cos0 * cos_j, sin0 * sin_j, sin0 * cos_j, cos0 * sin_j
+                    for pair in ((cc - ss, sc + cs), (cc + ss, sc - cs)):
+                        products.append(jnp.concatenate(pair, axis=1))
+                state = turned(state, turn)
             made.append(products)
-            moved = turned(state, (phase(2, at), phase(3, at)))
-            store([(state_ref, (q, at, slice(None)), moved[q]) for q in range(2)])
+            store([(state_ref, (q, at, slice(None)), state[q]) for q in range(2)])
         store([])
-        tiles = [jnp.concatenate([products[n] for products in made], axis=0) for n in range(8)]
+        return [
+            [jnp.concatenate([products[8 * n + m] for products in made], axis=0) for m in range(8)] for n in range(count)
+        ]
+
+    def dedisperse(b, tiles):
         found = [None] * 8
         for j in range(4):
             both = spec_ref[j, b]
@@ -332,9 +339,13 @@
             imag = jnp.where(move, pltpu.roll(imag, 8 - bit, 0), imag)
         part_ref[0, b] = real
         part_ref[1, b] = imag
+
+    def several(n, carry):
+        for m, tiles in enumerate(generate(AT_ONCE)):
+            dedisperse(n * AT_ONCE + m, tiles)
         return carry
 
-    lax.fori_loop(0, blocks, dedisperse, 0, unroll=8)
+    lax.fori_loop(0, blocks // AT_ONCE, several, 0, unroll=4)
 
     block = lax.broadcasted_iota(jnp.int32, (8, 128), 1) >> 3
     for half in range(lanes // 128):

time: 33.2 us -> 33 us (level)
  no operation moved by 1% of the time
where the time goes in v2:
time: 33 us; the launch traced here: 32.7 us
  Pallas kernels  11.1 us (34%)
  blocking collectives  9.48 us (29%)
  starting transfers between devices  7.4 us (22%)
  waiting for transfers between devices  3.96 us (12%)
  local copies, waits for them, and re-layouts  0.76 us (2%)
    all_to_all x1, blocking collectives, body(): got = lax.all_to_all(partial, 'wide', 0, 0, tiled=True)  9.48 us
    all_to_all x1, starting transfers between devices, body(): all_power = lax.all_to_all(power, 'wide', 0, 0, tiled=True)  7.4 us
    pallas_call x1, Pallas kernels, body(): call(main_kernel, shape((trials, 16, 128), BF16), [VMEM] * 3 + [HBM], [pl...  6.06 us
    all_to_all x1, waiting for transfers between devices, body(): all_power = lax.all_to_all(power, 'wide', 0, 0, tiled=True)  3.96 us
    pallas_call x1, Pallas kernels, body(): call(functools.partial(power_kernel, group), (shape((group, power_lanes),...  2.45 us
    pallas_call x1, Pallas kernels, body(): call(functools.partial(phase_kernel, group), (shape((HEAD + 8 * local, la...  1.6 us
    pallas_call x1, Pallas kernels, body(): call(functools.partial(inverse_kernel, group), shape((1, trials // group,...  0.96 us
    unnamed x8, local copies, waits for them, and re-layouts  0.76 us
  transfers between devices with their start and end apart: 1, of which 1 were waited for; matrix products, arithmetic and copies ran while one was open for 0% of the time, Pallas kernels for 5%

profile of v2, /device:TPU:0, one launch (start us, length us, event | category | flops | bytes accessed | tf_op | source)
XLA Modules:
  0.0 32.7 jit_solution(3295403469465329661)
XLA Ops:
  0.0 2.4 %band_power.1 = (f32[16,128]{1,0:T(8,128)}, f32[32,256]{1,0:T(8,128)}) custom-call(s32[7]{0:T(128)} %edges_hbm.1, s32[1,256]{1,0:T(1,128)} %bitcast.10, s32[16]{0:T(128)} %delays_hbm.1, bf16[256,4096]{1,0:T(8,128)(2,1)} %bitcast.7), custom_call_target="tpu_custom_call" | custom-call | tf_op jit(solution)/shard_map/band_power/pallas_call | solution.py:420
  2.5 7.4 %all-to-all-start = ((f32[16,1,128]{2,1,0:T(1,128)}), f32[16,1,128]{2,1,0:T(1,128)S(1)}, u32[]{:S(2)}, u32[]{:S(2)}) async-start(f32[16,1,128]{2,1,0:T(1,128)} %bitcast.9), calls=%async_computation | async-start | bytes 16384 | tf_op jit(solution)/shard_map/all_to_all | solution.py:436
  9.9 0.0 copy-start.1
  9.9 0.7 %copy-done.1 = f32[32,256]{1,0:T(8,128)S(1)} copy-done((f32[32,256]{1,0:T(8,128)S(1)}, f32[32,256]{1,0:T(8,128)}, u32[]{:S(2)}) %copy-start.1) | copy-done | bytes 32792
  10.6 1.6 %phases.1 = (f32[2072,128]{1,0:T(8,128)S(1)}, bf16[256,4096]{1,0:T(8,128)(2,1)S(1)}) custom-call(f32[32,256]{1,0:T(8,128)S(1)} %copy-done.1, bf16[256,4096]{1,0:T(8,128)(2,1)} %bitcast.8), custom_call_target="tpu_custom_call" | custom-call | tf_op jit(solution)/shard_map/phases/pallas_call | solution.py:438
  12.2 4.0 %all-to-all-done = f32[16,1,128]{2,1,0:T(1,128)S(1)} async-done(((f32[16,1,128]{2,1,0:T(1,128)}), f32[16,1,128]{2,1,0:T(1,128)S(1)}, u32[]{:S(2)}, u32[]{:S(2)}) %all-to-all-start) | async-done | bytes 8224 | tf_op jit(solution)/shard_map/all_to_all | solution.py:436
  16.2 0.0 copy-start
  16.2 0.0 copy-start.2
  16.2 0.0 copy-start.3
  16.2 6.1 %dedisperse.1 = bf16[16,16,128]{2,1,0:T(8,128)(2,1)S(1)} custom-call(f32[16,128]{1,0:T(8,128)S(1)} %bitcast.6, bf16[256,4096]{1,0:T(8,128)(2,1)S(1)} %get-tuple-element.11.x_ref, f32[2072,128]{1,0:T(8,128)S(1)} %get-tuple-element.12.pack_ref, bf16[2048,512]{1,0:T(8,128)(2,1)} %constant.8.clone.table_hbm), custom_call_target="tpu_custom_call" | custom-call | tf_op jit(solution)/shard_map/dedisperse/pallas_call | solution.py:447
  22.3 9.5 %all_to_all.16.got_ref = bf16[16,16,128]{2,1,0:T(8,128)(2,1)S(1)} all-to-all(bf16[16,16,128]{2,1,0:T(8,128)(2,1)S(1)} %dedisperse.1), channel_id=1, replica_groups=mesh['beam'=2,'wide'=16] {'wide'}, dimensions={0} | all-to-all | bytes 131072 | tf_op jit(solution)/shard_map/all_to_all | solution.py:462
  31.7 0.0 copy-done
  31.7 0.0 copy-done.2
  31.7 0.0 copy-done.3
  31.8 1.0 %inverse.1 = f32[1,1,4096]{2,1,0:T(1,128)} custom-call(bf16[16,16,128]{2,1,0:T(8,128)(2,1)S(1)} %all_to_all.16.got_ref, bf16[2,128,1024]{2,1,0:T(8,128)(2,1)S(1)} %copy-done, f32[2,8,512]{2,1,0:T(8,128)S(1)} %copy-done.2, f32[8,16]{1,0:T(8,128)S(1)} %copy-done.3), custom_call_target="tpu_custom_call" | custom-call | tf_op jit(solution)/shard_map/inverse/pallas_call | solution.py:465
Async XLA Ops:
  2.5 13.7 %all-to-all-start = ((f32[16,1,128]{2,1,0:T(1,128)}), f32[16,1,128]{2,1,0:T(1,128)S(1)}, u32[]{:S(2)}, u32[]{:S(2)}) async-start(f32[16,1,128]{2,1,0:T(1,128)} %bitcast.9), calls=%async_computation | async-start | bytes 16384 | tf_op jit(solution)/shard_map/all_to_all | solution.py:436
  9.9 0.8 %copy-start.1 = (f32[32,256]{1,0:T(8,128)S(1)}, f32[32,256]{1,0:T(8,128)}, u32[]{:S(2)}) copy-start(f32[32,256]{1,0:T(8,128)} %get-tuple-element.10.info_ref) | copy-start | bytes 98308
  16.2 15.6 %copy-start = (bf16[2,128,1024]{2,1,0:T(8,128)(2,1)S(1)}, bf16[2,128,1024]{2,1,0:T(8,128)(2,1)}, u32[]{:S(2)}) copy-start(bf16[2,128,1024]{2,1,0:T(8,128)(2,1)} %constant.9.clone.first_ref) | copy-start | bytes 1572868
  16.2 15.6 %copy-start.2 = (f32[2,8,512]{2,1,0:T(8,128)S(1)}, f32[2,8,512]{2,1,0:T(8,128)}, u32[]{:S(2)}) copy-start(f32[2,8,512]{2,1,0:T(8,128)} %constant.10.clone.twiddle_ref) | copy-start | bytes 98308
  16.2 15.6 %copy-start.3 = (f32[8,16]{1,0:T(8,128)S(1)}, f32[8,16]{1,0:T(8,128)}, u32[]{:S(2)}) copy-start(f32[8,16]{1,0:T(8,128)} %constant.11.clone.last_ref) | copy-start | bytes 1540

commit v3 on v1

--- a/solution.py
+++ b/solution.py
@@ -72,7 +72,9 @@
     twiddle = (weight * np.stack([np.cos(angle), np.sin(angle)])).astype(np.float32)
     p = np.arange(8)[:, None]
     angle = 2.0 * np.pi * ((p * r.T) % 8) / 8
-    last = np.concatenate([np.cos(angle), -np.sin(angle)], 1).astype(np.float32)
+    exact = np.concatenate([np.cos(angle), -np.sin(angle)], 1)
+    high = exact.astype(ml_dtypes.bfloat16)
+    last = np.concatenate([high, high, (exact - high.astype(np.float64)).astype(ml_dtypes.bfloat16)], 1)
     return first, twiddle, last
 
 
@@ -374,7 +376,9 @@
         imag = y[0:8, step:] + y[8:16, :step]
         cos, sin = twiddle_ref[0], twiddle_ref[1]
         z = jnp.concatenate([real * cos - imag * sin, real * sin + imag * cos], axis=0)
-        series = jnp.dot(last_ref[...], z, precision=lax.Precision.HIGHEST, preferred_element_type=F32)
+        high = z.astype(BF16)
+        low = (z - high.astype(F32)).astype(BF16)
+        series = jnp.dot(last_ref[...], jnp.concatenate([high, low, high], axis=0), preferred_element_type=F32)
         for p in range(8):
             out_ref[0, d : d + 1, p * step : (p + 1) * step] = series[p : p + 1, :]
 

time: 33.2 us -> 33.2 us (level)
  no operation moved by 1% of the time
where the time goes in v3:
time: 33.2 us; the launch traced here: 32.9 us
  Pallas kernels  11.2 us (34%)
  blocking collectives  9.48 us (29%)
  starting transfers between devices  7.4 us (22%)
  waiting for transfers between devices  3.96 us (12%)
  local copies, waits for them, and re-layouts  0.76 us (2%)
    all_to_all x1, blocking collectives, body(): got = lax.all_to_all(partial, 'wide', 0, 0, tiled=True)  9.48 us
    all_to_all x1, starting transfers between devices, body(): all_power = lax.all_to_all(power, 'wide', 0, 0, tiled=True)  7.4 us
    pallas_call x1, Pallas kernels, body(): call(main_kernel, shape((trials, 16, 128), BF16), [VMEM] * 3 + [HBM], [pl...  6.22 us
    all_to_all x1, waiting for transfers between devices, body(): all_power = lax.all_to_all(power, 'wide', 0, 0, tiled=True)  3.96 us
    pallas_call x1, Pallas kernels, body(): call(functools.partial(power_kernel, group), (shape((group, power_lanes),...  2.45 us
    pallas_call x1, Pallas kernels, body(): call(functools.partial(phase_kernel, group), (shape((HEAD + 8 * local, la...  1.6 us
    pallas_call x1, Pallas kernels, body(): call(functools.partial(inverse_kernel, group), shape((1, trials // group,...  0.94 us
    unnamed x8, local copies, waits for them, and re-layouts  0.76 us
  transfers between devices with their start and end apart: 1, of which 1 were waited for; matrix products, arithmetic and copies ran while one was open for 0% of the time, Pallas kernels for 5%

profile of v3, /device:TPU:0, one launch (start us, length us, event | category | flops | bytes accessed | tf_op | source)
XLA Modules:
  0.0 32.9 jit_solution(9455637624995357792)
XLA Ops:
  0.0 2.4 %band_power.1 = (f32[16,128]{1,0:T(8,128)}, f32[32,256]{1,0:T(8,128)}) custom-call(s32[7]{0:T(128)} %edges_hbm.1, s32[1,256]{1,0:T(1,128)} %bitcast.10, s32[16]{0:T(128)} %delays_hbm.1, bf16[256,4096]{1,0:T(8,128)(2,1)} %bitcast.7), custom_call_target="tpu_custom_call" | custom-call | tf_op jit(solution)/shard_map/band_power/pallas_call | solution.py:413
  2.5 7.4 %all-to-all-start = ((f32[16,1,128]{2,1,0:T(1,128)}), f32[16,1,128]{2,1,0:T(1,128)S(1)}, u32[]{:S(2)}, u32[]{:S(2)}) async-start(f32[16,1,128]{2,1,0:T(1,128)} %bitcast.9), calls=%async_computation | async-start | bytes 16384 | tf_op jit(solution)/shard_map/all_to_all | solution.py:429
  9.9 0.0 copy-start.1
  9.9 0.7 %copy-done.1 = f32[32,256]{1,0:T(8,128)S(1)} copy-done((f32[32,256]{1,0:T(8,128)S(1)}, f32[32,256]{1,0:T(8,128)}, u32[]{:S(2)}) %copy-start.1) | copy-done | bytes 32792
  10.6 1.6 %phases.1 = (f32[2072,128]{1,0:T(8,128)S(1)}, bf16[256,4096]{1,0:T(8,128)(2,1)S(1)}) custom-call(f32[32,256]{1,0:T(8,128)S(1)} %copy-done.1, bf16[256,4096]{1,0:T(8,128)(2,1)} %bitcast.8), custom_call_target="tpu_custom_call" | custom-call | tf_op jit(solution)/shard_map/phases/pallas_call | solution.py:431
  12.2 4.0 %all-to-all-done = f32[16,1,128]{2,1,0:T(1,128)S(1)} async-done(((f32[16,1,128]{2,1,0:T(1,128)}), f32[16,1,128]{2,1,0:T(1,128)S(1)}, u32[]{:S(2)}, u32[]{:S(2)}) %all-to-all-start) | async-done | bytes 8224 | tf_op jit(solution)/shard_map/all_to_all | solution.py:429
  16.2 0.0 copy-start
  16.2 0.0 copy-start.2
  16.2 0.0 copy-start.3
  16.2 6.2 %dedisperse.1 = bf16[16,16,128]{2,1,0:T(8,128)(2,1)S(1)} custom-call(f32[16,128]{1,0:T(8,128)S(1)} %bitcast.6, bf16[256,4096]{1,0:T(8,128)(2,1)S(1)} %get-tuple-element.11.x_ref, f32[2072,128]{1,0:T(8,128)S(1)} %get-tuple-element.12.pack_ref, bf16[2048,512]{1,0:T(8,128)(2,1)} %constant.8.clone.table_hbm), custom_call_target="tpu_custom_call" | custom-call | tf_op jit(solution)/shard_map/dedisperse/pallas_call | solution.py:440
  22.4 9.5 %all_to_all.16.got_ref = bf16[16,16,128]{2,1,0:T(8,128)(2,1)S(1)} all-to-all(bf16[16,16,128]{2,1,0:T(8,128)(2,1)S(1)} %dedisperse.1), channel_id=1, replica_groups=mesh['beam'=2,'wide'=16] {'wide'}, dimensions={0} | all-to-all | bytes 131072 | tf_op jit(solution)/shard_map/all_to_all | solution.py:455
  31.9 0.0 copy-done
  31.9 0.0 copy-done.2
  31.9 0.0 copy-done.3
  31.9 0.9 %inverse.1 = f32[1,1,4096]{2,1,0:T(1,128)} custom-call(bf16[16,16,128]{2,1,0:T(8,128)(2,1)S(1)} %all_to_all.16.got_ref, bf16[2,128,1024]{2,1,0:T(8,128)(2,1)S(1)} %copy-done, f32[2,8,512]{2,1,0:T(8,128)S(1)} %copy-done.2, bf16[8,48]{1,0:T(8,128)(2,1)S(1)} %copy-done.3), custom_call_target="tpu_custom_call" | custom-call | tf_op jit(solution)/shard_map/inverse/pallas_call | solution.py:458
Async XLA Ops:
  2.5 13.7 %all-to-all-start = ((f32[16,1,128]{2,1,0:T(1,128)}), f32[16,1,128]{2,1,0:T(1,128)S(1)}, u32[]{:S(2)}, u32[]{:S(2)}) async-start(f32[16,1,128]{2,1,0:T(1,128)} %bitcast.9), calls=%async_computation | async-start | bytes 16384 | tf_op jit(solution)/shard_map/all_to_all | solution.py:429
  9.9 0.8 %copy-start.1 = (f32[32,256]{1,0:T(8,128)S(1)}, f32[32,256]{1,0:T(8,128)}, u32[]{:S(2)}) copy-start(f32[32,256]{1,0:T(8,128)} %get-tuple-element.10.info_ref) | copy-start | bytes 98308
  16.2 15.7 %copy-start = (bf16[2,128,1024]{2,1,0:T(8,128)(2,1)S(1)}, bf16[2,128,1024]{2,1,0:T(8,128)(2,1)}, u32[]{:S(2)}) copy-start(bf16[2,128,1024]{2,1,0:T(8,128)(2,1)} %constant.9.clone.first_ref) | copy-start | bytes 1572868
  16.2 15.7 %copy-start.2 = (f32[2,8,512]{2,1,0:T(8,128)S(1)}, f32[2,8,512]{2,1,0:T(8,128)}, u32[]{:S(2)}) copy-start(f32[2,8,512]{2,1,0:T(8,128)} %constant.10.clone.twiddle_ref) | copy-start | bytes 98308
  16.2 15.7 %copy-start.3 = (bf16[8,48]{1,0:T(8,128)(2,1)S(1)}, bf16[8,48]{1,0:T(8,128)(2,1)}, u32[]{:S(2)}) copy-start(bf16[8,48]{1,0:T(8,128)(2,1)} %constant.11.clone.last_ref) | copy-start | bytes 2308

commit v4 on v2

--- a/solution.py
+++ b/solution.py
@@ -12,7 +12,7 @@
 
 NBLK = 8
 HEAD = 3 * NBLK
-AT_ONCE = 4
+AT_ONCE = 2
 F32 = jnp.float32
 BF16 = jnp.bfloat16
 VMEM = pl.BlockSpec(memory_space=pltpu.VMEM)
@@ -215,7 +215,7 @@
         )
         for n in range(8)
     ]
-    for n in (0, 4, 1, 7, 2, 6, 3, 5):
+    for n in range(8):
         table_copies[n].start()
     power = jnp.sum(power_ref[...], axis=0, keepdims=True)
     wide = power.shape[1]
@@ -345,7 +345,7 @@
             dedisperse(n * AT_ONCE + m, tiles)
         return carry
 
-    lax.fori_loop(0, blocks // AT_ONCE, several, 0, unroll=4)
+    lax.fori_loop(0, blocks // AT_ONCE, several, 0, unroll=8)
 
     block = lax.broadcasted_iota(jnp.int32, (8, 128), 1) >> 3
     for half in range(lanes // 128):

time: 33 us -> 33 us (level)
  no operation moved by 1% of the time
where the time goes in v4:
time: 33 us; the launch traced here: 32.7 us
  Pallas kernels  11.1 us (34%)
  blocking collectives  9.48 us (29%)
  starting transfers between devices  7.4 us (22%)
  waiting for transfers between devices  3.96 us (12%)
  local copies, waits for them, and re-layouts  0.76 us (2%)
    all_to_all x1, blocking collectives, body(): got = lax.all_to_all(partial, 'wide', 0, 0, tiled=True)  9.48 us
    all_to_all x1, starting transfers between devices, body(): all_power = lax.all_to_all(power, 'wide', 0, 0, tiled=True)  7.4 us
    pallas_call x1, Pallas kernels, body(): call(main_kernel, shape((trials, 16, 128), BF16), [VMEM] * 3 + [HBM], [pl...  6.05 us
    all_to_all x1, waiting for transfers between devices, body(): all_power = lax.all_to_all(power, 'wide', 0, 0, tiled=True)  3.96 us
    pallas_call x1, Pallas kernels, body(): call(functools.partial(power_kernel, group), (shape((group, power_lanes),...  2.45 us
    pallas_call x1, Pallas kernels, body(): call(functools.partial(phase_kernel, group), (shape((HEAD + 8 * local, la...  1.6 us
    pallas_call x1, Pallas kernels, body(): call(functools.partial(inverse_kernel, group), shape((1, trials // group,...  0.96 us
    unnamed x8, local copies, waits for them, and re-layouts  0.76 us
  transfers between devices with their start and end apart: 1, of which 1 were waited for; matrix products, arithmetic and copies ran while one was open for 0% of the time, Pallas kernels for 5%

profile of v4, /device:TPU:0, one launch (start us, length us, event | category | flops | bytes accessed | tf_op | source)
XLA Modules:
  0.0 32.7 jit_solution(8014949043727545115)
XLA Ops:
  0.0 2.4 %band_power.1 = (f32[16,128]{1,0:T(8,128)}, f32[32,256]{1,0:T(8,128)}) custom-call(s32[7]{0:T(128)} %edges_hbm.1, s32[1,256]{1,0:T(1,128)} %bitcast.10, s32[16]{0:T(128)} %delays_hbm.1, bf16[256,4096]{1,0:T(8,128)(2,1)} %bitcast.7), custom_call_target="tpu_custom_call" | custom-call | tf_op jit(solution)/shard_map/band_power/pallas_call | solution.py:420
  2.5 7.4 %all-to-all-start = ((f32[16,1,128]{2,1,0:T(1,128)}), f32[16,1,128]{2,1,0:T(1,128)S(1)}, u32[]{:S(2)}, u32[]{:S(2)}) async-start(f32[16,1,128]{2,1,0:T(1,128)} %bitcast.9), calls=%async_computation | async-start | bytes 16384 | tf_op jit(solution)/shard_map/all_to_all | solution.py:436
  9.9 0.0 copy-start.1
  9.9 0.7 %copy-done.1 = f32[32,256]{1,0:T(8,128)S(1)} copy-done((f32[32,256]{1,0:T(8,128)S(1)}, f32[32,256]{1,0:T(8,128)}, u32[]{:S(2)}) %copy-start.1) | copy-done | bytes 32792
  10.6 1.6 %phases.1 = (f32[2072,128]{1,0:T(8,128)S(1)}, bf16[256,4096]{1,0:T(8,128)(2,1)S(1)}) custom-call(f32[32,256]{1,0:T(8,128)S(1)} %copy-done.1, bf16[256,4096]{1,0:T(8,128)(2,1)} %bitcast.8), custom_call_target="tpu_custom_call" | custom-call | tf_op jit(solution)/shard_map/phases/pallas_call | solution.py:438
  12.2 4.0 %all-to-all-done = f32[16,1,128]{2,1,0:T(1,128)S(1)} async-done(((f32[16,1,128]{2,1,0:T(1,128)}), f32[16,1,128]{2,1,0:T(1,128)S(1)}, u32[]{:S(2)}, u32[]{:S(2)}) %all-to-all-start) | async-done | bytes 8224 | tf_op jit(solution)/shard_map/all_to_all | solution.py:436
  16.2 0.0 copy-start
  16.2 0.0 copy-start.2
  16.2 0.0 copy-start.3
  16.2 6.1 %dedisperse.1 = bf16[16,16,128]{2,1,0:T(8,128)(2,1)S(1)} custom-call(f32[16,128]{1,0:T(8,128)S(1)} %bitcast.6, bf16[256,4096]{1,0:T(8,128)(2,1)S(1)} %get-tuple-element.11.x_ref, f32[2072,128]{1,0:T(8,128)S(1)} %get-tuple-element.12.pack_ref, bf16[2048,512]{1,0:T(8,128)(2,1)} %constant.8.clone.table_hbm), custom_call_target="tpu_custom_call" | custom-call | tf_op jit(solution)/shard_map/dedisperse/pallas_call | solution.py:447
  22.3 9.5 %all_to_all.16.got_ref = bf16[16,16,128]{2,1,0:T(8,128)(2,1)S(1)} all-to-all(bf16[16,16,128]{2,1,0:T(8,128)(2,1)S(1)} %dedisperse.1), channel_id=1, replica_groups=mesh['beam'=2,'wide'=16] {'wide'}, dimensions={0} | all-to-all | bytes 131072 | tf_op jit(solution)/shard_map/all_to_all | solution.py:462
  31.7 0.0 copy-done
  31.7 0.0 copy-done.2
  31.7 0.0 copy-done.3
  31.7 1.0 %inverse.1 = f32[1,1,4096]{2,1,0:T(1,128)} custom-call(bf16[16,16,128]{2,1,0:T(8,128)(2,1)S(1)} %all_to_all.16.got_ref, bf16[2,128,1024]{2,1,0:T(8,128)(2,1)S(1)} %copy-done, f32[2,8,512]{2,1,0:T(8,128)S(1)} %copy-done.2, f32[8,16]{1,0:T(8,128)S(1)} %copy-done.3), custom_call_target="tpu_custom_call" | custom-call | tf_op jit(solution)/shard_map/inverse/pallas_call | solution.py:465
Async XLA Ops:
  2.5 13.7 %all-to-all-start = ((f32[16,1,128]{2,1,0:T(1,128)}), f32[16,1,128]{2,1,0:T(1,128)S(1)}, u32[]{:S(2)}, u32[]{:S(2)}) async-start(f32[16,1,128]{2,1,0:T(1,128)} %bitcast.9), calls=%async_computation | async-start | bytes 16384 | tf_op jit(solution)/shard_map/all_to_all | solution.py:436
  9.9 0.8 %copy-start.1 = (f32[32,256]{1,0:T(8,128)S(1)}, f32[32,256]{1,0:T(8,128)}, u32[]{:S(2)}) copy-start(f32[32,256]{1,0:T(8,128)} %get-tuple-element.10.info_ref) | copy-start | bytes 98308
  16.2 15.5 %copy-start = (bf16[2,128,1024]{2,1,0:T(8,128)(2,1)S(1)}, bf16[2,128,1024]{2,1,0:T(8,128)(2,1)}, u32[]{:S(2)}) copy-start(bf16[2,128,1024]{2,1,0:T(8,128)(2,1)} %constant.9.clone.first_ref) | copy-start | bytes 1572868
  16.2 15.5 %copy-start.2 = (f32[2,8,512]{2,1,0:T(8,128)S(1)}, f32[2,8,512]{2,1,0:T(8,128)}, u32[]{:S(2)}) copy-start(f32[2,8,512]{2,1,0:T(8,128)} %constant.10.clone.twiddle_ref) | copy-start | bytes 98308
  16.2 15.5 %copy-start.3 = (f32[8,16]{1,0:T(8,128)S(1)}, f32[8,16]{1,0:T(8,128)}, u32[]{:S(2)}) copy-start(f32[8,16]{1,0:T(8,128)} %constant.11.clone.last_ref) | copy-start | bytes 1540
